TPU v7x, 32 devices: a whole 2x2x4 slice. The times are simulated.
32 devices in a mesh: rep: 2 (over x), shard: 16 (over z, y, core).
Axes of the slice: x: 2, y: 2, z: 4, core: 2. Of those that a mesh axis runs over, the one named last changes fastest.
Arguments:
- tokens: bfloat16 [4096, 768], P(('rep', 'shard')), may hold values from -6 to 6
- cotangent: bfloat16 [4096, 768], P(('rep', 'shard')), may hold values from -6 to 6
- lengths: int32 [32, 3], P(('rep', 'shard')), may hold values from 1 to 96, 128 in all within a row
- routes: int32 [4096, 1], P(('rep', 'shard')), may hold values from 0 to 1; in each aligned block of 128 rows (0 to 127, 128 to 255, ...) at most 80 rows name the same one
- bucket_ids: int32 [255], replicated, may hold values from 0 to 31
- attn_in: bfloat16 [3, 768, 768], P(None, 'shard'), may hold values from -0.21875 to 0.21875
- attn_out: bfloat16 [768, 768], P('shard'), may hold values from -0.875 to 0.875
- gains: bfloat16 [2, 768], P(None, 'shard'), may hold values from 0.25 to 1.75
- router: bfloat16 [768, 2], P('shard'), may hold values from -0.109375 to 0.109375
- rel_table: bfloat16 [32, 12], P('shard'), may hold values from -4 to 4
- expert_in: bfloat16 [2, 768, 3072], P(None, 'shard'), may hold values from -0.21875 to 0.21875
- expert_out: bfloat16 [2, 3072, 768], P(None, 'shard'), may hold values from -0.21875 to 0.21875
Outputs:
- layer_out: bfloat16 [4096, 768], P(('rep', 'shard'))
- input_grad: float32 [4096, 768], P(('rep', 'shard'))
- grad_attn_in: float32 [3, 768, 768], P(None, 'shard')
- grad_attn_out: float32 [768, 768], P('shard')
- grad_gains: float32 [2, 768], P(None, 'shard')
- grad_router: float32 [768, 2], P('shard')
- grad_rel_table: float32 [32, 12], P('shard')
- grad_expert_in: float32 [2, 768, 3072], P(None, 'shard')
- grad_expert_out: float32 [2, 3072, 768], P(None, 'shard')
Inputs may be any that keep to these rules, and one draw needn't show every extreme that they name: Row b holds the lengths of the 3 sequences of device block b; they sum to 128, and some block has one of exactly 96. `routes`: within the 128 rows of one device no expert is named more than 80 times, and in every draw some device names some expert exactly 80 times.
All inputs are finite; a program needn't handle non-finite values.
Results may differ from a plain program's by a relative error of at most 0.012.
Values may be sent and summed in bfloat16 or wider, within the bound.
A program may use at most 192 MiB of HBM per device.

v0:
```python
import jax
import jax.numpy as jnp
from jax import lax
from jax.sharding import PartitionSpec as P

BUCKETS = 32
CAP = 80
epsilon = 1e-06


def rms_norm(values, gain):
    return values * lax.rsqrt(jnp.mean(values * values, axis=-1, keepdims=True) + epsilon) * gain


def gelu_tanh(values):
    return jax.nn.gelu(values, approximate=True)


def offsets_to_pairs(per_offset, length):
    heads = per_offset.shape[0]
    reverse = per_offset[:, ::-1]
    repeated = jnp.broadcast_to(reverse[:, None, :], (heads, length, 2 * length - 1))
    repeated = repeated.reshape(heads, length * (2 * length - 1))
    repeated = jnp.pad(repeated, ((0, 0), (0, length)))
    skewed = repeated.reshape(heads, length, 2 * length)[:, :, :length]
    return skewed[:, :, ::-1]


def pairs_to_offsets(grid, length):
    heads = grid.shape[0]
    flipped = grid[:, :, ::-1]
    padded = jnp.pad(flipped, ((0, 0), (0, 0), (0, length)))
    flat = padded.reshape(heads, 2 * length * length)[:, : length * (2 * length - 1)]
    skewed = flat.reshape(heads, length, 2 * length - 1)
    return jnp.sum(skewed, axis=1)[:, ::-1]


def shards(
    tokens,
    cotangent,
    lengths,
    routes,
    bucket_ids,
    attn_in,
    attn_out,
    gains,
    router,
    rel_table,
    expert_in,
    expert_out,
):
    highest = lax.Precision.HIGHEST
    length = tokens.shape[0]
    width = tokens.shape[1]
    heads = rel_table.shape[1]
    head_size = width // heads
    experts = expert_in.shape[0]
    capacity = CAP
    bucket_count = BUCKETS
    full_in, full_out, full_gains, full_router, full_table = (
        lax.all_gather(attn_in, "shard", axis=1, tiled=True),
        lax.all_gather(attn_out, "shard", axis=0, tiled=True),
        lax.all_gather(gains, "shard", axis=1, tiled=True),
        lax.all_gather(router, "shard", axis=0, tiled=True),
        lax.all_gather(rel_table, "shard", axis=0, tiled=True),
    )
    inputs = tokens.astype(jnp.float32)
    gain_attn = full_gains[0].astype(jnp.float32)
    gain_ffn = full_gains[1].astype(jnp.float32)
    normed = rms_norm(inputs, gain_attn).astype(jnp.bfloat16)
    projected = jnp.einsum(
        "td,kde->kte", normed, full_in, preferred_element_type=jnp.float32
    ).astype(jnp.bfloat16)
    query = projected[0].reshape(length, heads, head_size)
    keys = projected[1].reshape(length, heads, head_size)
    values = projected[2].reshape(length, heads, head_size)
    places = jnp.arange(length, dtype=jnp.int32)
    offset_onehot = (
        bucket_ids[:, None] == jnp.arange(bucket_count, dtype=jnp.int32)[None, :]
    ).astype(jnp.float32)
    offset_bias = jnp.einsum(
        "ob,bh->ho", offset_onehot, full_table.astype(jnp.float32), precision=highest
    )
    bias = offsets_to_pairs(offset_bias, length)
    ends = jnp.cumsum(lengths[0])
    segment = jnp.sum((places[:, None] >= ends[None, :]).astype(jnp.int32), axis=1)
    allowed = segment[:, None] == segment[None, :]

    def masked_scores():
        raw = jnp.einsum("qhc,khc->hqk", query, keys, preferred_element_type=jnp.float32) * 0.125
        return jnp.where(allowed[None], raw + bias, -1e30)

    scores = masked_scores()
    peak = jnp.max(scores, axis=-1, keepdims=True)
    expo = jnp.exp(scores - peak)
    totals = jnp.sum(expo, axis=-1, keepdims=True)
    logsum = peak + jnp.log(totals)
    probs_low = (expo / totals).astype(jnp.bfloat16)
    context = jnp.einsum("hqk,khc->qhc", probs_low, values, preferred_element_type=jnp.float32)
    context = context.astype(jnp.bfloat16).reshape(length, width)
    hidden = inputs + jnp.dot(context, full_out, preferred_element_type=jnp.float32)
    normed_ffn = rms_norm(hidden, gain_ffn).astype(jnp.bfloat16)
    logits = jnp.dot(normed_ffn, full_router, preferred_element_type=jnp.float32)
    gate_probs = jax.nn.softmax(logits, axis=-1)
    chosen = routes[:, 0]
    picked = chosen[:, None] == jnp.arange(experts, dtype=jnp.int32)[None, :]
    gate = jnp.sum(jnp.where(picked, gate_probs, 0.0), axis=1)
    ranks = jnp.cumsum(picked.astype(jnp.int32), axis=0) - 1
    slot = chosen * capacity + jnp.sum(jnp.where(picked, ranks, 0), axis=1)
    dispatch = (jnp.arange(experts * capacity, dtype=jnp.int32)[:, None] == slot[None, :]).astype(
        jnp.bfloat16
    )
    buffers = jnp.dot(dispatch, normed_ffn, preferred_element_type=jnp.float32).astype(jnp.bfloat16)
    buffers = buffers.reshape(experts, capacity, width)
    before_list = []
    active_list = []
    returned_list = []
    for expert in range(experts):
        batch = buffers[expert]
        whole_in = lax.all_gather(expert_in[expert], "shard", axis=0, tiled=True)
        before = jnp.dot(batch, whole_in, preferred_element_type=jnp.float32)
        active = gelu_tanh(before).astype(jnp.bfloat16)
        whole_out = lax.all_gather(expert_out[expert], "shard", axis=0, tiled=True)
        returned = jnp.dot(active, whole_out, preferred_element_type=jnp.float32)
        before_list.append(before)
        active_list.append(active)
        returned_list.append(returned)
    returned_all = jnp.concatenate(returned_list, axis=0)
    gathered = jnp.take(returned_all, slot, axis=0)
    layer_out = (hidden + gate[:, None] * gathered).astype(jnp.bfloat16)
    upstream = cotangent.astype(jnp.float32)
    gate_grad = jnp.sum(upstream * gathered, axis=1)
    scaled = (gate[:, None] * upstream).astype(jnp.bfloat16)
    returned_grad = jnp.dot(dispatch, scaled, preferred_element_type=jnp.float32).astype(
        jnp.bfloat16
    )
    returned_grad = returned_grad.reshape(experts, capacity, width)
    batch_grads = []
    inner_shards = []
    outer_shards = []
    for expert in range(experts):
        batch = buffers[expert]
        active = active_list[expert]
        out_grad = returned_grad[expert]
        out_matrix = lax.all_gather(expert_out[expert], "shard", axis=0, tiled=True)
        active_grad = jnp.einsum(
            "cd,fd->cf", out_grad, out_matrix, preferred_element_type=jnp.float32
        )
        before_grad = jax.vjp(gelu_tanh, before_list[expert])[1](active_grad)[0].astype(
            jnp.bfloat16
        )
        in_matrix = lax.all_gather(expert_in[expert], "shard", axis=0, tiled=True)
        batch_grad = jnp.einsum(
            "cf,df->cd", before_grad, in_matrix, preferred_element_type=jnp.float32
        )
        batch_grads.append(batch_grad)
        inner_shard = lax.psum_scatter(
            jnp.einsum("cd,cf->df", batch, before_grad, preferred_element_type=jnp.float32),
            "shard",
            scatter_dimension=0,
            tiled=True,
        )
        outer_shard = lax.psum_scatter(
            jnp.einsum("cf,cd->fd", active, out_grad, preferred_element_type=jnp.float32),
            "shard",
            scatter_dimension=0,
            tiled=True,
        )
        inner_shards.append(inner_shard)
        outer_shards.append(outer_shard)
    batch_all = jnp.concatenate(batch_grads, axis=0)
    ffn_normed_grad = jnp.take(batch_all, slot, axis=0)
    prob_grad = jnp.where(picked, gate_grad[:, None], 0.0)
    logit_grad = gate_probs * (prob_grad - jnp.sum(gate_probs * prob_grad, axis=1, keepdims=True))
    normed_wide = normed_ffn.astype(jnp.float32)
    router_grad = jnp.einsum("td,te->de", normed_wide, logit_grad, precision=highest)
    ffn_normed_grad = ffn_normed_grad + jnp.einsum(
        "te,de->td", logit_grad, full_router.astype(jnp.float32), precision=highest
    )
    norm_pull = jax.vjp(rms_norm, hidden, gain_ffn)[1]
    hidden_from_norm, gain_ffn_grad = norm_pull(ffn_normed_grad)
    hidden_grad = upstream + hidden_from_norm
    attn_grad = hidden_grad.astype(jnp.bfloat16)
    attn_out_grad = jnp.einsum("td,te->de", context, attn_grad, preferred_element_type=jnp.float32)
    context_grad = jnp.einsum("te,de->td", attn_grad, full_out, preferred_element_type=jnp.float32)
    context_grad = context_grad.astype(jnp.bfloat16).reshape(length, heads, head_size)
    probs = jnp.exp(masked_scores() - logsum)
    probs_back = probs.astype(jnp.bfloat16)
    prob_grad_attn = jnp.einsum(
        "qhc,khc->hqk", context_grad, values, preferred_element_type=jnp.float32
    )
    value_grad = jnp.einsum(
        "hqk,qhc->khc", probs_back, context_grad, preferred_element_type=jnp.float32
    )
    score_grad = probs * (prob_grad_attn - jnp.sum(probs * prob_grad_attn, axis=-1, keepdims=True))
    offset_grad = pairs_to_offsets(score_grad, length)
    table_grad = jnp.einsum("ho,ob->bh", offset_grad, offset_onehot, precision=highest)
    score_low = score_grad.astype(jnp.bfloat16)
    query_grad = (
        jnp.einsum("hqk,khc->qhc", score_low, keys, preferred_element_type=jnp.float32) * 0.125
    )
    key_grad = (
        jnp.einsum("hqk,qhc->khc", score_low, query, preferred_element_type=jnp.float32) * 0.125
    )
    projected_grad = jnp.stack(
        [
            query_grad.reshape(length, width),
            key_grad.reshape(length, width),
            value_grad.reshape(length, width),
        ]
    ).astype(jnp.bfloat16)
    attn_in_grad = jnp.einsum(
        "td,kte->kde", normed, projected_grad, preferred_element_type=jnp.float32
    )
    normed_grad = jnp.einsum(
        "kte,kde->td", projected_grad, full_in, preferred_element_type=jnp.float32
    )
    input_pull = jax.vjp(rms_norm, inputs, gain_attn)[1]
    input_from_norm, gain_attn_grad = input_pull(normed_grad)
    input_grad = hidden_grad + input_from_norm
    gains_grad = jnp.stack([gain_attn_grad, gain_ffn_grad])
    in_shard, out_shard, gains_shard, router_shard, table_shard = (
        lax.psum_scatter(attn_in_grad, "shard", scatter_dimension=1, tiled=True),
        lax.psum_scatter(attn_out_grad, "shard", scatter_dimension=0, tiled=True),
        lax.psum_scatter(gains_grad, "shard", scatter_dimension=1, tiled=True),
        lax.psum_scatter(router_grad, "shard", scatter_dimension=0, tiled=True),
        lax.psum_scatter(table_grad, "shard", scatter_dimension=0, tiled=True),
    )
    expert_in_grad = jnp.stack(inner_shards)
    expert_out_grad = jnp.stack(outer_shards)
    in_shard, out_shard, gains_shard, router_shard, table_shard, expert_in_grad, expert_out_grad = (
        lax.psum(
            (
                in_shard,
                out_shard,
                gains_shard,
                router_shard,
                table_shard,
                expert_in_grad,
                expert_out_grad,
            ),
            "rep",
        )
    )
    return (
        layer_out,
        input_grad,
        in_shard,
        out_shard,
        gains_shard,
        router_shard,
        table_shard,
        expert_in_grad,
        expert_out_grad,
    )


def solution(mesh):
    placed = (
        P(("rep", "shard"), None),
        P(("rep", "shard"), None),
        P(("rep", "shard"), None),
        P(("rep", "shard"), None),
        P(),
        P(None, "shard", None),
        P("shard", None),
        P(None, "shard"),
        P("shard", None),
        P("shard", None),
        P(None, "shard", None),
        P(None, "shard", None),
    )
    return jax.shard_map(
        shards,
        mesh=mesh,
        in_specs=placed,
        out_specs=(
            P(("rep", "shard"), None),
            P(("rep", "shard"), None),
            P(None, "shard", None),
            P("shard", None),
            P(None, "shard"),
            P("shard", None),
            P("shard", None),
            P(None, "shard", None),
            P(None, "shard", None),
        ),
        check_vma=False,
    )
```

profile of v0, /device:TPU:0, one launch (start us, length us, event | category | flops | bytes accessed | tf_op | source)
XLA Modules:
  0.0 1300.3 jit_solution(768440275594427823)
XLA Ops:
  13.8 23.2 %all-gather.4 = bf16[16,48,2]{1,2,0:T(2,128)(2,1)S(1)} all-gather(bf16[1,48,2]{1,2,0:T(2,128)(2,1)} %bitcast.144), channel_id=1, replica_groups=mesh['rep'=2,'shard'=16] {'shard'}, dimensions={0}, use_global_device_ids=true | all-gather | bytes 3264 | tf_op jit(solution)/shard_map/all_gather | solution.py:63
  37.1 17.5 %all-gather.6 = bf16[16,48,2]{1,2,0:T(2,128)(2,1)S(1)} all-gather(bf16[1,48,2]{1,2,0:T(2,128)(2,1)} %bitcast.145), channel_id=1, replica_groups=mesh['rep'=2,'shard'=16] {'shard'}, dimensions={0}, use_global_device_ids=true | all-gather | bytes 3264 | tf_op jit(solution)/shard_map/all_gather | solution.py:64
  54.7 18.9 %all-gather.5 = bf16[16,2,12]{2,1,0:T(2,128)(2,1)S(1)} all-gather(bf16[1,2,12]{2,1,0:T(2,128)(2,1)} %bitcast.146), channel_id=1, replica_groups=mesh['rep'=2,'shard'=16] {'shard'}, dimensions={0}, use_global_device_ids=true | all-gather | bytes 816 | tf_op jit(solution)/shard_map/all_gather | solution.py:65
  86.5 13.4 %all-gather.16.cloned.1.call-done = bf16[768,768]{1,0:T(8,128)(2,1)} async-done(((bf16[48,768]{1,0:T(8,128)(2,1)}), bf16[768,768]{1,0:T(8,128)(2,1)}) %all-gather.16.cloned.1.call-update) | async-done | bytes 1179664 | tf_op jit(solution)/shard_map/all_gather | solution.py:62
  103.0 51.6 %all-gather.22.cloned.1.call-done = bf16[1,768,3072]{2,1,0:T(8,128)(2,1)} async-done(((bf16[1,48,3072]{2,1,0:T(8,128)(2,1)}), bf16[1,768,3072]{2,1,0:T(8,128)(2,1)}) %all-gather.22.cloned.1.call-update) | async-done | bytes 4718608 | tf_op jit(solution)/shard_map/all_gather | solution.py:120
  157.9 51.4 %all-gather.18.cloned.1.call-done = bf16[1,768,3072]{2,1,0:T(8,128)(2,1)} async-done(((bf16[1,48,3072]{2,1,0:T(8,128)(2,1)}), bf16[1,768,3072]{2,1,0:T(8,128)(2,1)}) %all-gather.18.cloned.1.call-update) | async-done | bytes 4718608 | tf_op jit(solution)/shard_map/all_gather | solution.py:120
  212.6 51.4 %all-gather.24.cloned.1.call-done = bf16[1,3072,768]{2,1,0:T(8,128)(2,1)} async-done(((bf16[1,192,768]{2,1,0:T(8,128)(2,1)}), bf16[1,3072,768]{2,1,0:T(8,128)(2,1)}) %all-gather.24.cloned.1.call-update) | async-done | bytes 4718608 | tf_op jit(solution)/shard_map/all_gather | solution.py:123
  268.0 50.7 %all-gather.20.cloned.1.call-done = bf16[1,3072,768]{2,1,0:T(8,128)(2,1)} async-done(((bf16[1,192,768]{2,1,0:T(8,128)(2,1)}), bf16[1,3072,768]{2,1,0:T(8,128)(2,1)}) %all-gather.20.cloned.1.call-update) | async-done | bytes 4718608 | tf_op jit(solution)/shard_map/all_gather | solution.py:123
  326.5 4.1 fusion.34
  357.0 11.0 copy.96
  369.2 5.7 fusion.67
  375.9 5.1 fusion.64
  381.9 5.1 fusion.61
  387.1 5.0 fusion.58
  402.0 149.6 %all-reduce.9.cloned.1.call-done = f32[3,768,768]{2,0,1:T(4,128)} async-done(((f32[3,768,768]{2,0,1:T(4,128)}), f32[3,768,768]{2,0,1:T(4,128)}) %all-reduce.9.cloned.1.call-update) | async-done | bytes 7077904
  553.6 114.1 %reduce-scatter.14.cloned.1.call-done = f32[48,3072]{1,0:T(8,128)} async-done(((f32[768,3072]{1,0:T(8,128)}), f32[48,3072]{1,0:T(8,128)}) %reduce-scatter.14.cloned.1.call-update) | async-done | bytes 589840 | tf_op jit(solution)/shard_map/reduce_scatter | solution.py:157
  667.6 115.2 %reduce-scatter.16.cloned.1.call-done = f32[48,3072]{1,0:T(8,128)} async-done(((f32[768,3072]{1,0:T(8,128)}), f32[48,3072]{1,0:T(8,128)}) %reduce-scatter.16.cloned.1.call-update) | async-done | bytes 589840 | tf_op jit(solution)/shard_map/reduce_scatter | solution.py:157
  785.2 113.3 %reduce-scatter.18.cloned.1.call-done = f32[192,768]{1,0:T(8,128)} async-done(((f32[3072,768]{1,0:T(8,128)}), f32[192,768]{1,0:T(8,128)}) %reduce-scatter.18.cloned.1.call-update) | async-done | bytes 589840 | tf_op jit(solution)/shard_map/reduce_scatter | solution.py:163
  898.6 115.2 %reduce-scatter.20.cloned.1.call-done = f32[192,768]{1,0:T(8,128)} async-done(((f32[3072,768]{1,0:T(8,128)}), f32[192,768]{1,0:T(8,128)}) %reduce-scatter.20.cloned.1.call-update) | async-done | bytes 589840 | tf_op jit(solution)/shard_map/reduce_scatter | solution.py:163
  1016.1 64.5 %reduce-scatter.12.cloned.1.call-done = f32[48,768]{1,0:T(8,128)} async-done(((f32[768,768]{1,0:T(8,128)}), f32[48,768]{1,0:T(8,128)}) %reduce-scatter.12.cloned.1.call-update) | async-done | bytes 147472 | tf_op jit(solution)/shard_map/reduce_scatter | solution.py:224
  1089.3 57.6 %all-reduce.3 = f32[32,12]{1,0:T(8,128)S(1)} all-reduce(f32[32,12]{1,0:T(8,128)S(1)} %fusion.75), channel_id=10, replica_groups=mesh['rep'=2,'shard'=16] {'shard'}, use_global_device_ids=true, to_apply=%region_27.29.clone | all-reduce | flops 384 | bytes 3072
  1148.7 49.0 %reduce-scatter.24.cloned.1.call-done = f32[48,2]{1,0:T(8,128)} async-done(((f32[768,2]{1,0:T(8,128)}), f32[48,2]{1,0:T(8,128)}) %reduce-scatter.24.cloned.1.call-update) | async-done | bytes 400
  1198.5 5.5 all-reduce.4
  1204.0 81.5 %all-reduce.11.cloned.1.call-done = (f32[3,48,768]{2,0,1:T(4,128)}, f32[48,768]{1,0:T(8,128)}, f32[2,48,3072]{2,1,0:T(8,128)}, f32[2,192,768]{2,1,0:T(8,128)}) async-done(((f32[3,48,768]{2,0,1:T(4,128)}, f32[48,768]{1,0:T(8,128)}, f32[2,48,3072]{2,1,0:T(8,128)}, f32[2,192,768]{2,1,0:T(8,128)}), (f32[3,48,768]{2,0,1:T(4,128)}, f32[48,768]{1,0:T(8,128)}, f32[2,48,3072]{2,1,0:T(8,128)}, ...) | async-done | bytes 2949136 | tf_op jit(solution)/shard_map/psum | solution.py:232
  (205 shorter events, 104.5 us)
Async XLA Ops:
  7.2 75.3 %all-gather.14.cloned.1.call-start = ((), (), s32[]{:S(2)}) async-start(), calls=%async_computation.7 | async-start | bytes 3760128 | tf_op jit(solution)/shard_map/all_gather | solution.py:61
  7.9 92.0 %all-gather.16.cloned.1.call-start = ((), (), s32[]{:S(2)}) async-start(), calls=%async_computation.8 | async-start | bytes 1253376 | tf_op jit(solution)/shard_map/all_gather | solution.py:62
  8.7 146.0 %all-gather.22.cloned.1.call-start = ((), (), s32[]{:S(2)}) async-start(), calls=%async_computation.16 | async-start | bytes 5013504 | tf_op jit(solution)/shard_map/all_gather | solution.py:120
  10.6 198.7 %all-gather.18.cloned.1.call-start = ((), (), s32[]{:S(2)}) async-start(), calls=%async_computation.14 | async-start | bytes 5013504 | tf_op jit(solution)/shard_map/all_gather | solution.py:120
  11.2 252.8 %all-gather.24.cloned.1.call-start = ((), (), s32[]{:S(2)}) async-start(), calls=%async_computation.17 | async-start | bytes 5013504 | tf_op jit(solution)/shard_map/all_gather | solution.py:123
  13.2 305.5 %all-gather.20.cloned.1.call-start = ((), (), s32[]{:S(2)}) async-start(), calls=%async_computation.15 | async-start | bytes 5013504 | tf_op jit(solution)/shard_map/all_gather | solution.py:123
  13.8 537.8 %all-reduce.9.cloned.1.call-start = ((), (), s32[]{:S(2)}) async-start(), calls=%async_computation.20 | async-start | bytes 18874368
  85.4 16.3 %copy-start.13 = (bf16[1,128,768]{1,2,0:T(8,128)(2,1)}, bf16[1,128,768]{1,2,0:T(8,128)(2,1)S(1)}, u32[]{:S(2)}) copy-start(bf16[1,128,768]{1,2,0:T(8,128)(2,1)S(1)} %copy.82) | copy-start | bytes 589828
  85.6 17.2 %copy-start.14 = (bf16[1,128,768]{1,2,0:T(8,128)(2,1)}, bf16[1,128,768]{1,2,0:T(8,128)(2,1)S(1)}, u32[]{:S(2)}) copy-start(bf16[1,128,768]{1,2,0:T(8,128)(2,1)S(1)} %copy.81) | copy-start | bytes 589828
  85.7 72.2 %copy-start.20 = (bf16[1,128,768]{1,2,0:T(8,128)(2,1)}, bf16[1,128,768]{1,2,0:T(8,128)(2,1)S(1)}, u32[]{:S(2)}) copy-start(bf16[1,128,768]{1,2,0:T(8,128)(2,1)S(1)} %copy.80) | copy-start | bytes 589828
  86.5 16.5 %copy-start.18 = (bf16[12,64,128]{2,1,0:T(8,128)(2,1)}, bf16[12,64,128]{2,1,0:T(8,128)(2,1)S(1)}, u32[]{:S(2)}) copy-start(bf16[12,64,128]{2,1,0:T(8,128)(2,1)S(1)} %convolution_convert_fusion.5) | copy-start | bytes 589828
  102.5 110.1 %copy-start.5 = (bf16[128,768]{1,0:T(8,128)(2,1)}, bf16[128,768]{1,0:T(8,128)(2,1)S(1)}, u32[]{:S(2)}) copy-start(bf16[128,768]{1,0:T(8,128)(2,1)S(1)} %multiply_convert_fusion.2) | copy-start | bytes 589828
  103.0 109.6 %copy-start.7 = (bf16[160,768]{1,0:T(8,128)(2,1)}, bf16[160,768]{1,0:T(8,128)(2,1)S(1)}, u32[]{:S(2)}) copy-start(bf16[160,768]{1,0:T(8,128)(2,1)S(1)} %convolution_convert_fusion.2) | copy-start | bytes 737284
  323.7 7.0 copy-start.4
  326.5 7.4 slice-start.2
  368.1 299.6 %reduce-scatter.14.cloned.1.call-start = ((), (), s32[]{:S(2)}) async-start(), calls=%async_computation.10 | async-start | bytes 10027008 | tf_op jit(solution)/shard_map/reduce_scatter | solution.py:157
  374.9 408.0 %reduce-scatter.16.cloned.1.call-start = ((), (), s32[]{:S(2)}) async-start(), calls=%async_computation.11 | async-start | bytes 10027008 | tf_op jit(solution)/shard_map/reduce_scatter | solution.py:157
  381.0 517.5 %reduce-scatter.18.cloned.1.call-start = ((), (), s32[]{:S(2)}) async-start(), calls=%async_computation.12 | async-start | bytes 10027008 | tf_op jit(solution)/shard_map/reduce_scatter | solution.py:163
  387.0 626.8 %reduce-scatter.20.cloned.1.call-start = ((), (), s32[]{:S(2)}) async-start(), calls=%async_computation.13 | async-start | bytes 10027008 | tf_op jit(solution)/shard_map/reduce_scatter | solution.py:163
  392.1 688.5 %reduce-scatter.12.cloned.1.call-start = ((), (), s32[]{:S(2)}) async-start(), calls=%async_computation.9 | async-start | bytes 2506752 | tf_op jit(solution)/shard_map/reduce_scatter | solution.py:224
  394.8 753.0 %reduce-scatter.22.cloned.1.call-start = ((), (), s32[]{:S(2)}) async-start(), calls=%async_computation.18 | async-start | bytes 417792
  400.7 797.0 %reduce-scatter.24.cloned.1.call-start = ((), (), s32[]{:S(2)}) async-start(), calls=%async_computation.19 | async-start | bytes 417792
  401.9 679.4 %copy-start.1 = (f32[12,128,128]{1,2,0:T(8,128)S(1)}, f32[12,128,128]{1,2,0:T(8,128)}, u32[]{:S(2)}) copy-start(f32[12,128,128]{1,2,0:T(8,128)} %copy-done) | copy-start | bytes 2359300
  401.9 883.6 %all-reduce.11.cloned.1.call-start = ((), (), s32[]{:S(2)}) async-start(), calls=%async_computation.21 | async-start | bytes 6193152 | tf_op jit(solution)/shard_map/psum | solution.py:232
  (25 other events, 75.7 us)
Sparse Core Ops, SparseCore 0:
  10.3 49.9 all-gather.13
  62.6 37.3 all-gather.15
  102.2 52.3 all-gather.21
  157.3 51.9 all-gather.17
  212.0 51.9 all-gather.23
  266.7 51.9 all-gather.19
  368.2 183.3 all-reduce.8
  556.2 111.3 reduce-scatter.13
  671.8 111.0 reduce-scatter.15
  787.4 111.1 reduce-scatter.17
  902.7 111.0 reduce-scatter.19
  1017.9 62.7 reduce-scatter.11
  1084.7 54.5 reduce-scatter.21
  1143.1 54.5 reduce-scatter.23
  1201.2 84.2 all-reduce.10
where the time goes:
time: 1300 us
  waiting for transfers between devices  1020 us (78%)
  blocking collectives  123 us (9%)
  matrix products  72.4 us (6%)
  local copies, waits for them, and re-layouts  51.6 us (4%)
  between operations  16 us (1%)
  other arithmetic  13.3 us (1%)
    reduce_scatter x2, waiting for transfers between devices, shards(): lax.psum_scatter(jnp.einsum('cd,cf->df', batch, before_grad, preferred_el...  229 us
    reduce_scatter x2, waiting for transfers between devices, shards(): lax.psum_scatter(jnp.einsum('cf,cd->fd', active, out_grad, preferred_elem...  229 us
    unnamed x18, waiting for transfers between devices  201 us
    all_gather x2, waiting for transfers between devices, shards(): whole_in = lax.all_gather(expert_in[expert], 'shard', axis=0, tiled=True)  103 us
    all_gather x2, waiting for transfers between devices, shards(): whole_out = lax.all_gather(expert_out[expert], 'shard', axis=0, tiled=True)  102 us
    psum x1, waiting for transfers between devices, shards(): lax.psum((in_shard, out_shard, gains_shard, router_shard, table_shard, ex...  81.5 us
    reduce_scatter x1, waiting for transfers between devices, shards(): lax.psum_scatter(attn_out_grad, 'shard', scatter_dimension=0, tiled=True)  64.5 us
    unnamed x1, blocking collectives  57.6 us
  transfers between devices with their start and end apart: 15, of which 13 were waited for; matrix products, arithmetic and copies ran while one was open for 6% of the time, Pallas kernels for 0%

commit v1 on v0

--- a/solution.py
+++ b/solution.py
@@ -6,6 +6,28 @@
 BUCKETS = 32
 CAP = 80
 epsilon = 1e-06
+
+
+def in_order(pieces, dim):
+    pieces = jnp.moveaxis(pieces, 0, dim)
+    shape = pieces.shape
+    return pieces.reshape(*shape[:dim], shape[dim] * shape[dim + 1], *shape[dim + 2 :])
+
+
+def collected_by_bits(value, axis):
+    size = lax.axis_size(axis)
+    blocks = value[None]
+    for level in range(size.bit_length() - 1):
+        bit = 1 << level
+        theirs = lax.ppermute(blocks, axis, [(i, i ^ bit) for i in range(size)])
+        both = jnp.stack([blocks, theirs])
+        upper = lax.axis_index(axis) >> level & 1
+        blocks = jnp.where(upper == 0, both, both[::-1]).reshape(-1, *value.shape)
+    return blocks
+
+
+def collect(shard, axis, dim):
+    return in_order(collected_by_bits(shard, axis), dim)
 
 
 def rms_norm(values, gain):
@@ -117,7 +139,7 @@
     returned_list = []
     for expert in range(experts):
         batch = buffers[expert]
-        whole_in = lax.all_gather(expert_in[expert], "shard", axis=0, tiled=True)
+        whole_in = collect(expert_in[expert], "shard", 0)
         before = jnp.dot(batch, whole_in, preferred_element_type=jnp.float32)
         active = gelu_tanh(before).astype(jnp.bfloat16)
         whole_out = lax.all_gather(expert_out[expert], "shard", axis=0, tiled=True)

time: 1300 us -> 1480 us (1.14)
  blocking collectives: 123 us -> 207 us
  waiting for transfers between devices: 1020 us -> 1080 us
  other arithmetic: 13.3 us -> 28.7 us
    ppermute x0 -> x8, waiting for transfers between devices: none -> 158 us  [collected_by_bits(): theirs = lax.ppermute(blocks, axis, [(i, i ^ bit) for i in range(size)])]
    all_gather x2, waiting for transfers between devices: 102 us -> 27.6 us  [shards(): whole_out = lax.all_gather(expert_out[expert], 'shard', axis=0, tiled=True)]
    all_gather x1, blocking collectives: 17.5 us -> 72.9 us  [shards(): lax.all_gather(router, 'shard', axis=0, tiled=True)]
    all_gather x1, blocking collectives: 23.2 us -> 53.4 us  [shards(): lax.all_gather(gains, 'shard', axis=1, tiled=True)]
    all_gather x2, waiting for transfers between devices: 103 us -> 87.1 us  [shards(): in_matrix = lax.all_gather(expert_in[expert], 'shard', axis=0, tiled=True)]
  transfers between devices with their start and end apart: 15 -> 23, of which waited for: 13 -> 16; matrix products, arithmetic and copies ran while one was open for 6% -> 8% of each run, Pallas kernels for 0% -> 0%
where the time goes in v1:
time: 1480 us; the launch traced here: 1470 us
  waiting for transfers between devices  1080 us (73%)
  blocking collectives  207 us (14%)
  matrix products  76.9 us (5%)
  local copies, waits for them, and re-layouts  61.3 us (4%)
  other arithmetic  28.7 us (2%)
  between operations  16.3 us (1%)
    reduce_scatter x2, waiting for transfers between devices, shards(): lax.psum_scatter(jnp.einsum('cd,cf->df', batch, before_grad, preferred_el...  229 us
    reduce_scatter x2, waiting for transfers between devices, shards(): lax.psum_scatter(jnp.einsum('cf,cd->fd', active, out_grad, preferred_elem...  229 us
    unnamed x18, waiting for transfers between devices  201 us
    ppermute x8, waiting for transfers between devices, collected_by_bits(): theirs = lax.ppermute(blocks, axis, [(i, i ^ bit) for i in range(size)])  158 us
    all_gather x2, waiting for transfers between devices, shards(): in_matrix = lax.all_gather(expert_in[expert], 'shard', axis=0, tiled=True)  87.1 us
    psum x1, waiting for transfers between devices, shards(): lax.psum((in_shard, out_shard, gains_shard, router_shard, table_shard, ex...  81.5 us
    all_gather x1, blocking collectives, shards(): lax.all_gather(router, 'shard', axis=0, tiled=True)  72.9 us
    reduce_scatter x1, waiting for transfers between devices, shards(): lax.psum_scatter(attn_out_grad, 'shard', scatter_dimension=0, tiled=True)  64.5 us
  transfers between devices with their start and end apart: 23, of which 16 were waited for; matrix products, arithmetic and copies ran while one was open for 8% of the time, Pallas kernels for 0%

profile of v1, /device:TPU:0, one launch (start us, length us, event | category | flops | bytes accessed | tf_op | source)
XLA Modules:
  0.0 1474.1 jit_solution(1930658653076004595)
XLA Ops:
  17.6 16.2 %collective-permute-done.1 = bf16[2,48,3072]{2,1,0:T(8,128)(2,1)S(1)} collective-permute-done((bf16[2,48,3072]{2,1,0:T(8,128)(2,1)S(1)}, bf16[2,48,3072]{2,1,0:T(8,128)(2,1)S(1)}, u32[]{:S(2)}, u32[]{:S(2)}) %collective-permute-start.1) | collective-permute-done | bytes 589856 | tf_op jit(solution)/shard_map/ppermute | solution.py:22
  36.4 53.4 %all-gather.4 = bf16[16,48,2]{1,2,0:T(2,128)(2,1)S(1)} all-gather(bf16[1,48,2]{1,2,0:T(2,128)(2,1)S(1)} %bitcast.189), channel_id=1, replica_groups=mesh['rep'=2,'shard'=16] {'shard'}, dimensions={0}, use_global_device_ids=true | all-gather | bytes 3264 | tf_op jit(solution)/shard_map/all_gather | solution.py:85
  89.9 17.6 %all-gather.5 = bf16[16,2,12]{2,1,0:T(2,128)(2,1)S(1)} all-gather(bf16[1,2,12]{2,1,0:T(2,128)(2,1)S(1)} %bitcast.190), channel_id=1, replica_groups=mesh['rep'=2,'shard'=16] {'shard'}, dimensions={0}, use_global_device_ids=true | all-gather | bytes 816 | tf_op jit(solution)/shard_map/all_gather | solution.py:87
  110.0 59.6 %collective-permute-done.6 = bf16[4,48,3072]{2,1,0:T(8,128)(2,1)S(1)} collective-permute-done((bf16[4,48,3072]{2,1,0:T(8,128)(2,1)S(1)}, bf16[4,48,3072]{2,1,0:T(8,128)(2,1)S(1)}, u32[]{:S(2)}, u32[]{:S(2)}) %collective-permute-start.6) | collective-permute-done | bytes 1179680 | tf_op jit(solution)/shard_map/ppermute | solution.py:22
  181.1 6.8 rev.37
  188.4 72.9 %all-gather.6 = bf16[16,48,2]{1,2,0:T(2,128)(2,1)S(1)} all-gather(bf16[1,48,2]{1,2,0:T(2,128)(2,1)S(1)} %bitcast.191), channel_id=1, replica_groups=mesh['rep'=2,'shard'=16] {'shard'}, dimensions={0}, use_global_device_ids=true | all-gather | bytes 3264 | tf_op jit(solution)/shard_map/all_gather | solution.py:86
  261.8 32.8 %collective-permute-done.3 = bf16[8,48,3072]{2,1,0:T(8,128)(2,1)} collective-permute-done((bf16[8,48,3072]{2,1,0:T(8,128)(2,1)S(1)}, bf16[8,48,3072]{2,1,0:T(8,128)(2,1)}, u32[]{:S(2)}, u32[]{:S(2)}) %collective-permute-start.3) | collective-permute-done | bytes 2359328 | tf_op jit(solution)/shard_map/ppermute | solution.py:22
  296.8 47.9 %collective-permute-done.7 = bf16[8,48,3072]{2,1,0:T(8,128)(2,1)} collective-permute-done((bf16[8,48,3072]{2,1,0:T(8,128)(2,1)}, bf16[8,48,3072]{2,1,0:T(8,128)(2,1)}, u32[]{:S(2)}, u32[]{:S(2)}) %collective-permute-start.7) | collective-permute-done | bytes 2359328 | tf_op jit(solution)/shard_map/ppermute | solution.py:22
  371.7 27.5 %all-gather.20.cloned.1.call-done = bf16[1,3072,768]{2,1,0:T(8,128)(2,1)} async-done(((bf16[1,192,768]{2,1,0:T(8,128)(2,1)}), bf16[1,3072,768]{2,1,0:T(8,128)(2,1)}) %all-gather.20.cloned.1.call-update) | async-done | bytes 4718608 | tf_op jit(solution)/shard_map/all_gather | solution.py:145
  411.5 41.8 %all-gather.22.cloned.1.call-done = bf16[1,768,3072]{2,1,0:T(8,128)(2,1)} async-done(((bf16[1,48,3072]{2,1,0:T(8,128)(2,1)}), bf16[1,768,3072]{2,1,0:T(8,128)(2,1)}) %all-gather.22.cloned.1.call-update) | async-done | bytes 4718608 | tf_op jit(solution)/shard_map/all_gather | solution.py:174
  462.1 45.3 %all-gather.24.cloned.1.call-done = bf16[1,768,3072]{2,1,0:T(8,128)(2,1)} async-done(((bf16[1,48,3072]{2,1,0:T(8,128)(2,1)}), bf16[1,768,3072]{2,1,0:T(8,128)(2,1)}) %all-gather.24.cloned.1.call-update) | async-done | bytes 4718608 | tf_op jit(solution)/shard_map/all_gather | solution.py:174
  531.9 11.0 copy.104
  544.1 5.7 fusion.68
  556.8 5.1 fusion.61
  577.2 149.3 %all-reduce.9.cloned.1.call-done = f32[3,768,768]{2,0,1:T(4,128)} async-done(((f32[3,768,768]{2,0,1:T(4,128)}), f32[3,768,768]{2,0,1:T(4,128)}) %all-reduce.9.cloned.1.call-update) | async-done | bytes 7077904
  728.4 114.1 %reduce-scatter.14.cloned.1.call-done = f32[48,3072]{1,0:T(8,128)} async-done(((f32[768,3072]{1,0:T(8,128)}), f32[48,3072]{1,0:T(8,128)}) %reduce-scatter.14.cloned.1.call-update) | async-done | bytes 589840 | tf_op jit(solution)/shard_map/reduce_scatter | solution.py:179
  842.5 115.2 %reduce-scatter.16.cloned.1.call-done = f32[48,3072]{1,0:T(8,128)} async-done(((f32[768,3072]{1,0:T(8,128)}), f32[48,3072]{1,0:T(8,128)}) %reduce-scatter.16.cloned.1.call-update) | async-done | bytes 589840 | tf_op jit(solution)/shard_map/reduce_scatter | solution.py:179
  960.1 113.3 %reduce-scatter.18.cloned.1.call-done = f32[192,768]{1,0:T(8,128)} async-done(((f32[3072,768]{1,0:T(8,128)}), f32[192,768]{1,0:T(8,128)}) %reduce-scatter.18.cloned.1.call-update) | async-done | bytes 589840 | tf_op jit(solution)/shard_map/reduce_scatter | solution.py:185
  1073.4 115.2 %reduce-scatter.20.cloned.1.call-done = f32[192,768]{1,0:T(8,128)} async-done(((f32[3072,768]{1,0:T(8,128)}), f32[192,768]{1,0:T(8,128)}) %reduce-scatter.20.cloned.1.call-update) | async-done | bytes 589840 | tf_op jit(solution)/shard_map/reduce_scatter | solution.py:185
  1191.1 64.5 %reduce-scatter.12.cloned.1.call-done = f32[48,768]{1,0:T(8,128)} async-done(((f32[768,768]{1,0:T(8,128)}), f32[48,768]{1,0:T(8,128)}) %reduce-scatter.12.cloned.1.call-update) | async-done | bytes 147472 | tf_op jit(solution)/shard_map/reduce_scatter | solution.py:246
  1263.9 57.6 %all-reduce.3 = f32[32,12]{1,0:T(8,128)S(1)} all-reduce(f32[32,12]{1,0:T(8,128)S(1)} %fusion.77), channel_id=10, replica_groups=mesh['rep'=2,'shard'=16] {'shard'}, use_global_device_ids=true, to_apply=%region_27.29.clone | all-reduce | flops 384 | bytes 3072
  1323.3 49.3 %reduce-scatter.24.cloned.1.call-done = f32[48,2]{1,0:T(8,128)} async-done(((f32[768,2]{1,0:T(8,128)}), f32[48,2]{1,0:T(8,128)}) %reduce-scatter.24.cloned.1.call-update) | async-done | bytes 400
  1373.4 5.5 all-reduce.4
  1378.9 81.5 %all-reduce.11.cloned.1.call-done = (f32[3,48,768]{2,0,1:T(4,128)}, f32[48,768]{1,0:T(8,128)}, f32[2,48,3072]{2,1,0:T(8,128)}, f32[2,192,768]{2,1,0:T(8,128)}) async-done(((f32[3,48,768]{2,0,1:T(4,128)}, f32[48,768]{1,0:T(8,128)}, f32[2,48,3072]{2,1,0:T(8,128)}, f32[2,192,768]{2,1,0:T(8,128)}), (f32[3,48,768]{2,0,1:T(4,128)}, f32[48,768]{1,0:T(8,128)}, f32[2,48,3072]{2,1,0:T(8,128)}, ...) | async-done | bytes 2949136 | tf_op jit(solution)/shard_map/psum | solution.py:254
  (253 shorter events, 148.5 us)
Async XLA Ops:
  7.2 347.1 %all-gather.14.cloned.1.call-start = ((), (), s32[]{:S(2)}) async-start(), calls=%async_computation.7 | async-start | bytes 3760128 | tf_op jit(solution)/shard_map/all_gather | solution.py:83
  7.9 350.5 %all-gather.16.cloned.1.call-start = ((), (), s32[]{:S(2)}) async-start(), calls=%async_computation.8 | async-start | bytes 1253376 | tf_op jit(solution)/shard_map/all_gather | solution.py:84
  8.7 359.0 %all-gather.18.cloned.1.call-start = ((), (), s32[]{:S(2)}) async-start(), calls=%async_computation.14 | async-start | bytes 5013504 | tf_op jit(solution)/shard_map/all_gather | solution.py:145
  10.6 388.6 %all-gather.20.cloned.1.call-start = ((), (), s32[]{:S(2)}) async-start(), calls=%async_computation.15 | async-start | bytes 5013504 | tf_op jit(solution)/shard_map/all_gather | solution.py:145
  11.2 442.1 %all-gather.22.cloned.1.call-start = ((), (), s32[]{:S(2)}) async-start(), calls=%async_computation.16 | async-start | bytes 5013504 | tf_op jit(solution)/shard_map/all_gather | solution.py:174
  12.2 495.3 %all-gather.24.cloned.1.call-start = ((), (), s32[]{:S(2)}) async-start(), calls=%async_computation.17 | async-start | bytes 5013504 | tf_op jit(solution)/shard_map/all_gather | solution.py:174
  12.2 1.9 collective-permute-start
  12.7 4.5 collective-permute-start.4
  14.3 19.4 %collective-permute-start.1 = (bf16[2,48,3072]{2,1,0:T(8,128)(2,1)S(1)}, bf16[2,48,3072]{2,1,0:T(8,128)(2,1)S(1)}, u32[]{:S(2)}, u32[]{:S(2)}) collective-permute-start(bf16[2,48,3072]{2,1,0:T(8,128)(2,1)S(1)} %get-tuple-element.65), channel_id=1, source_target_pairs={{0,2},{1,3},{2,0},{3,1},{4,6},{5,7},{6,4},{7,5},{8,10},{9,11},{10,... | collective-permute-start | bytes 1769480 | tf_op jit(solution)/shard_map/ppermute | solution.py:22
  17.5 90.0 %collective-permute-start.5 = (bf16[2,48,3072]{2,1,0:T(8,128)(2,1)S(1)}, bf16[2,48,3072]{2,1,0:T(8,128)(2,1)}, u32[]{:S(2)}, u32[]{:S(2)}) collective-permute-start(bf16[2,48,3072]{2,1,0:T(8,128)(2,1)S(1)} %get-tuple-element.73), channel_id=1, source_target_pairs={{0,2},{1,3},{2,0},{3,1},{4,6},{5,7},{6,4},{7,5},{8,10},{9,11},{10,... | collective-permute-start | bytes 1769480 | tf_op jit(solution)/shard_map/ppermute | solution.py:22
  34.1 74.9 %collective-permute-start.2 = (bf16[4,48,3072]{2,1,0:T(8,128)(2,1)S(1)}, bf16[4,48,3072]{2,1,0:T(8,128)(2,1)S(1)}, u32[]{:S(2)}, u32[]{:S(2)}) collective-permute-start(bf16[4,48,3072]{2,1,0:T(8,128)(2,1)S(1)} %bitcast.151), channel_id=1, source_target_pairs={{0,4},{1,5},{2,6},{3,7},{4,0},{5,1},{6,2},{7,3},{8,12},{9,13},{10,... | collective-permute-start | bytes 3538952 | tf_op jit(solution)/shard_map/ppermute | solution.py:22
  36.3 690.1 %all-reduce.9.cloned.1.call-start = ((), (), s32[]{:S(2)}) async-start(), calls=%async_computation.20 | async-start | bytes 18874368
  109.0 60.6 %collective-permute-start.6 = (bf16[4,48,3072]{2,1,0:T(8,128)(2,1)S(1)}, bf16[4,48,3072]{2,1,0:T(8,128)(2,1)S(1)}, u32[]{:S(2)}, u32[]{:S(2)}) collective-permute-start(bf16[4,48,3072]{2,1,0:T(8,128)(2,1)S(1)} %bitcast.153), channel_id=1, source_target_pairs={{0,4},{1,5},{2,6},{3,7},{4,0},{5,1},{6,2},{7,3},{8,12},{9,13},{10,... | collective-permute-start | bytes 3538952 | tf_op jit(solution)/shard_map/ppermute | solution.py:22
  109.9 184.8 %collective-permute-start.3 = (bf16[8,48,3072]{2,1,0:T(8,128)(2,1)S(1)}, bf16[8,48,3072]{2,1,0:T(8,128)(2,1)}, u32[]{:S(2)}, u32[]{:S(2)}) collective-permute-start(bf16[8,48,3072]{2,1,0:T(8,128)(2,1)S(1)} %bitcast.146), channel_id=1, source_target_pairs={{0,8},{1,9},{2,10},{3,11},{4,12},{5,13},{6,14},{7,15},{8,0},{9,1},... | collective-permute-start | bytes 7077896 | tf_op jit(solution)/shard_map/ppermute | solution.py:22
  171.8 172.8 %collective-permute-start.7 = (bf16[8,48,3072]{2,1,0:T(8,128)(2,1)}, bf16[8,48,3072]{2,1,0:T(8,128)(2,1)}, u32[]{:S(2)}, u32[]{:S(2)}) collective-permute-start(bf16[8,48,3072]{2,1,0:T(8,128)(2,1)} %bitcast.41), channel_id=1, source_target_pairs={{0,8},{1,9},{2,10},{3,11},{4,12},{5,13},{6,14},{7,15},{8,0},{9,1},... | collective-permute-start | bytes 7077896 | tf_op jit(solution)/shard_map/ppermute | solution.py:22
  179.8 81.8 %copy-start.3 = (bf16[128,768]{1,0:T(8,128)(2,1)S(1)}, bf16[128,768]{1,0:T(8,128)(2,1)}, u32[]{:S(2)}) copy-start(bf16[128,768]{1,0:T(8,128)(2,1)} %param.14) | copy-start | bytes 589828
  542.9 299.6 %reduce-scatter.14.cloned.1.call-start = ((), (), s32[]{:S(2)}) async-start(), calls=%async_computation.10 | async-start | bytes 10027008 | tf_op jit(solution)/shard_map/reduce_scatter | solution.py:179
  549.8 408.0 %reduce-scatter.16.cloned.1.call-start = ((), (), s32[]{:S(2)}) async-start(), calls=%async_computation.11 | async-start | bytes 10027008 | tf_op jit(solution)/shard_map/reduce_scatter | solution.py:179
  555.9 517.5 %reduce-scatter.18.cloned.1.call-start = ((), (), s32[]{:S(2)}) async-start(), calls=%async_computation.12 | async-start | bytes 10027008 | tf_op jit(solution)/shard_map/reduce_scatter | solution.py:185
  561.9 626.7 %reduce-scatter.20.cloned.1.call-start = ((), (), s32[]{:S(2)}) async-start(), calls=%async_computation.13 | async-start | bytes 10027008 | tf_op jit(solution)/shard_map/reduce_scatter | solution.py:185
  567.1 688.5 %reduce-scatter.12.cloned.1.call-start = ((), (), s32[]{:S(2)}) async-start(), calls=%async_computation.9 | async-start | bytes 2506752 | tf_op jit(solution)/shard_map/reduce_scatter | solution.py:246
  569.8 752.7 %reduce-scatter.22.cloned.1.call-start = ((), (), s32[]{:S(2)}) async-start(), calls=%async_computation.18 | async-start | bytes 417792
  575.9 796.7 %reduce-scatter.24.cloned.1.call-start = ((), (), s32[]{:S(2)}) async-start(), calls=%async_computation.19 | async-start | bytes 417792
  577.1 883.3 %all-reduce.11.cloned.1.call-start = ((), (), s32[]{:S(2)}) async-start(), calls=%async_computation.21 | async-start | bytes 6193152 | tf_op jit(solution)/shard_map/psum | solution.py:254
  (42 other events, 343.0 us)
Sparse Core Ops, SparseCore 0:
  10.3 59.5 all-gather.13
  72.2 42.5 all-gather.15
  117.6 169.1 all-gather.17
  289.0 110.1 all-gather.19
  401.3 51.9 all-gather.21
  455.4 51.9 all-gather.23
  543.0 183.3 all-reduce.8
  731.1 111.3 reduce-scatter.13
  846.6 111.0 reduce-scatter.15
  962.3 111.1 reduce-scatter.17
  1077.5 111.0 reduce-scatter.19
  1192.8 62.7 reduce-scatter.11
  1259.6 54.5 reduce-scatter.21
  1318.0 54.5 reduce-scatter.23
  1376.1 84.2 all-reduce.10
